TPU v7x, 128 devices: a whole 4x4x4 slice. The times are simulated.
128 devices in a mesh: users: 64 (over z, y, x), mp: 2 (over core).
Axes of the slice: x: 4, y: 4, z: 4, core: 2. Of those that a mesh axis runs over, the one named last changes fastest.
Arguments:
- candidates: bfloat16 [65536, 1024], P('users', 'mp'), may hold values from -6 to 6
- cand_dest: int32 [65536, 1], P('users'), may hold values from 0 to 63; in each aligned block of 1024 rows (0 to 1023, 1024 to 2047, ...) at most 32 rows name the same one
- cand_slot: int32 [65536], P('users'), may hold values from 0 to 1
- hist_len: int32 [64, 2], P('users'), may hold values from 64 to 512, as said below
- k_cache: bfloat16 [128, 512, 1024], P('users', None, 'mp'), may hold values from -6 to 6
- v_cache: bfloat16 [128, 512, 1024], P('users', None, 'mp'), may hold values from -6 to 6
- in_gain: float32 [1024], replicated, may hold values from 0.25 to 1.75
- w_uvqk: bfloat16 [1024, 4, 1024], P(None, None, 'mp'), may hold values from -0.1875 to 0.1875
- attn_gain: float32 [1024], P('mp'), may hold values from 0.25 to 1.75
- w_out: bfloat16 [1024, 1024], P(None, 'mp'), may hold values from -0.1875 to 0.1875
Outputs:
- scored: bfloat16 [65536, 1024], P('users', 'mp')
Inputs may be any that keep to these rules, and one draw needn't show every extreme that they name: `cand_dest`: among the rows of one index of users, no owner is named by more than 32 rows, a bound that some block reaches. `hist_len`: for each owner, one of its 2 lengths is exactly 512.
All inputs are finite; a program needn't handle non-finite values.
Results may differ from a plain program's by a relative error of at most 0.0058.
Values may be sent and summed in bfloat16 or wider, within the bound.
A program may use at most 128 MiB of HBM per device.

v0:
```python
import math

import jax
import jax.numpy as jnp
from jax import lax
from jax.sharding import PartitionSpec as P

D = 1024
HD = 128
UPD = 2
HLEN = 512


def body(
    candidates, cand_dest, cand_slot, hist_len, k_cache, v_cache, in_gain, w_uvqk, attn_gain, w_out
):
    peers = lax.axis_size("users")
    width = candidates.shape[1]
    rows_here = candidates.shape[0]
    heads_here = width // HD
    scale = 1.0 / math.sqrt(HD)
    target = cand_dest[:, 0]
    onehot = (target[:, None] == jnp.arange(peers, dtype=jnp.int32)[None, :]).astype(jnp.bfloat16)
    row_ids = jnp.arange(rows_here, dtype=jnp.int32)
    earlier = (row_ids[:, None] > row_ids[None, :]).astype(jnp.bfloat16)
    before = jnp.dot(earlier, onehot, preferred_element_type=jnp.float32)
    position = jnp.sum(before * onehot.astype(jnp.float32), axis=1).astype(jnp.int32)
    cap_rows = max(2, 2 * rows_here // peers)
    slots_all = peers * cap_rows
    flat_slot = target * cap_rows + position
    dispatch = (jnp.arange(slots_all, dtype=jnp.int32)[:, None] == flat_slot[None, :]).astype(
        jnp.bfloat16
    )
    buffer = jnp.dot(dispatch, candidates, preferred_element_type=jnp.float32).astype(jnp.bfloat16)
    buffer = buffer.reshape(peers, cap_rows, candidates.shape[1])
    slot_plus = (cand_slot + 1).astype(jnp.float32)
    slot_flat = jnp.sum(dispatch.astype(jnp.float32) * slot_plus[None, :], axis=1) - 1.0
    slot_buf = slot_flat.reshape(peers, cap_rows).astype(jnp.bfloat16)
    lengths = hist_len[0]
    rows_in = lax.all_to_all(buffer, "users", split_axis=0, concat_axis=0, tiled=True)
    slots_in = lax.all_to_all(slot_buf, "users", split_axis=0, concat_axis=0, tiled=True)
    count_a, count_b = slots_in.shape
    total = count_a * count_b
    full_rows = lax.all_gather(rows_in, "mp", axis=2, tiled=True)
    xf = full_rows.reshape(total, D).astype(jnp.float32)
    mean_in = jnp.mean(xf, axis=-1, keepdims=True)
    var_in = jnp.mean((xf - mean_in) * (xf - mean_in), axis=-1, keepdims=True)
    normed = ((xf - mean_in) * lax.rsqrt(var_in + 1e-05) * in_gain).astype(jnp.bfloat16)
    proj = jnp.einsum("rd,dgc->rgc", normed, w_uvqk, preferred_element_type=jnp.float32)
    act = jax.nn.silu(proj).astype(jnp.bfloat16)
    query = act[:, 2].reshape(total, heads_here, HD)
    own_key = act[:, 3].reshape(total, heads_here, HD)
    own_val = act[:, 1].reshape(total, heads_here, HD)
    slot_int = slots_in.reshape(total).astype(jnp.int32)
    block = math.gcd(total, 256)

    def one_block(index):
        start = index * block
        query_b = lax.dynamic_slice_in_dim(query, start, block, 0)
        key_b = lax.dynamic_slice_in_dim(slot_int, start, block, 0)
        acc = jnp.zeros((block, heads_here, HD), jnp.float32)
        for user in range(UPD):

            def attend(acc_in, user=user):
                keys = k_cache[user].reshape(HLEN, heads_here, HD)
                vals = v_cache[user].reshape(HLEN, heads_here, HD)
                scores = (
                    jnp.einsum("rhc,phc->rhp", query_b, keys, preferred_element_type=jnp.float32)
                    * scale
                )
                valid = (jnp.arange(HLEN)[None, None, :] < lengths[user]) & (key_b == user)[
                    :, None, None
                ]
                wts = jnp.where(valid, jax.nn.silu(scores), 0.0).astype(jnp.bfloat16)
                return acc_in + jnp.einsum(
                    "rhp,phc->rhc", wts, vals, preferred_element_type=jnp.float32
                )

            touches = jnp.any(key_b == user)
            acc = lax.cond(touches, attend, lambda acc_in: acc_in, acc)
        return acc

    blocks_out = lax.map(one_block, jnp.arange(total // block, dtype=jnp.int32))
    summed = blocks_out.reshape(total, heads_here, HD)
    denom = jnp.ones((total,), jnp.float32)
    for user in range(UPD):
        denom = denom + jnp.where(slot_int == user, lengths[user].astype(jnp.float32), 0.0)
    self_w = jax.nn.silu(
        jnp.einsum("rhc,rhc->rh", query, own_key, preferred_element_type=jnp.float32) * scale
    ).astype(jnp.bfloat16)
    summed = summed + self_w.astype(jnp.float32)[:, :, None] * own_val.astype(jnp.float32)
    attn = (summed / denom[:, None, None]).reshape(total, width)
    row_sum, row_square = lax.psum((jnp.sum(attn, axis=-1), jnp.sum(attn * attn, axis=-1)), "mp")
    mean_at = row_sum / D
    var_at = row_square / D - mean_at * mean_at
    y_rows = (
        (attn - mean_at[:, None])
        * lax.rsqrt(var_at[:, None] + 1e-05)
        * attn_gain
        * act[:, 0].astype(jnp.float32)
    ).astype(jnp.bfloat16)
    y_rows = y_rows.reshape(count_a, count_b, width)
    projected = jnp.einsum(
        "abc,cd->abd",
        lax.all_gather(y_rows, "mp", axis=2, tiled=True),
        w_out,
        preferred_element_type=jnp.float32,
    )
    finished = (rows_in.astype(jnp.float32) + projected).astype(jnp.bfloat16)
    back = lax.all_to_all(finished, "users", split_axis=0, concat_axis=0, tiled=True)
    back_flat = back.reshape(slots_all, width)
    return jnp.einsum("sr,sw->rw", dispatch, back_flat, preferred_element_type=jnp.float32).astype(
        jnp.bfloat16
    )


def solution(mesh):
    return jax.shard_map(
        body,
        mesh=mesh,
        in_specs=(
            P("users", "mp"),
            P("users", None),
            P("users"),
            P("users", None),
            P("users", None, "mp"),
            P("users", None, "mp"),
            P(),
            P(None, None, "mp"),
            P("mp"),
            P(None, "mp"),
        ),
        out_specs=P("users", "mp"),
        check_vma=False,
    )
```

profile of v0, /device:TPU:1, one launch (start us, length us, event | category | flops | bytes accessed | tf_op | source)
XLA Modules:
  0.0 349.0 jit_solution(8795007122302137056)
XLA Ops:
  11.0 40.5 %all_to_all.16 = bf16[64,32,512]{2,1,0:T(8,128)(2,1)} all-to-all(bf16[64,32,512]{2,1,0:T(8,128)(2,1)S(1)} %bitcast.117), channel_id=1, replica_groups=mesh['users'=64,'mp'=2] {'users'}, dimensions={0} | all-to-all | bytes 4194304 | tf_op jit(solution)/shard_map/all_to_all | solution.py:40
  53.4 7.2 %all-to-all-start.1 = ((bf16[64,1,32]{2,1,0:T(2,128)(2,1)}), bf16[64,1,32]{2,1,0:T(2,128)(2,1)S(1)}, u32[]{:S(2)}, u32[]{:S(2)}) async-start(bf16[64,1,32]{2,1,0:T(2,128)(2,1)} %convert_element_type.173), calls=%async_computation.1 | async-start | bytes 65536 | tf_op jit(solution)/shard_map/all_to_all | solution.py:41
  64.8 4.2 %all-to-all-done.1 = bf16[64,1,32]{2,1,0:T(2,128)(2,1)S(1)} async-done(((bf16[64,1,32]{2,1,0:T(2,128)(2,1)}), bf16[64,1,32]{2,1,0:T(2,128)(2,1)S(1)}, u32[]{:S(2)}, u32[]{:S(2)}) %all-to-all-start.1) | async-done | bytes 4128 | tf_op jit(solution)/shard_map/all_to_all | solution.py:41
  81.1 11.6 %multiply_convert_fusion = bf16[2048,4,512]{2,0,1:T(8,128)(2,1)S(1)} fusion(bf16[2048,1024]{1,0:T(8,128)(2,1)S(1)} %fusion.32, bf16[1024,4,512]{2,1,0:T(4,128)(2,1)S(1)} %copy-done.11), kind=kOutput, calls=%fused_computation.44 | convolution fusion | flops 8610906112 | bytes 16777216 | tf_op jit(solution)/shard_map/rd,dgc->rgc/dot_general | solution.py:49
  92.7 4.1 %slice_convert_fusion = (f32[2048,1,512]{2,0,1:T(8,128)}, bf16[2048,1,512]{2,0,1:T(8,128)(2,1)}, bf16[2048,1,512]{2,0,1:T(8,128)(2,1)}, bf16[2048,1,512]{2,0,1:T(8,128)(2,1)}) fusion(bf16[2048,4,512]{2,0,1:T(8,128)(2,1)S(1)} %multiply_convert_fusion), kind=kLoop, calls=%fused_computation.73 | loop fusion | flops 1048576 | bytes 18874368 | tf_op jit(solution)/shard_map/convert_element_type | solution.py:91
  96.8 4.0 %reshape_squeeze.7 = bf16[2048,4,128]{2,1,0:T(4,128)(2,1)} reshape(bf16[2048,1,512]{2,0,1:T(8,128)(2,1)} %get-tuple-element.155) | data formatting | bytes 4194304 | tf_op jit(solution)/shard_map/reshape;squeeze | solution.py:51
  100.8 4.0 %reshape_squeeze.8 = bf16[2048,4,128]{2,1,0:T(4,128)(2,1)} reshape(bf16[2048,1,512]{2,0,1:T(8,128)(2,1)} %get-tuple-element.154) | data formatting | bytes 4194304 | tf_op jit(solution)/shard_map/reshape;squeeze | solution.py:52
  104.8 5.0 %fusion.37 = f32[2048,4]{1,0:T(8,128)S(1)} fusion(bf16[2048,4,128]{2,1,0:T(4,128)(2,1)} %reshape_squeeze.7, bf16[2048,4,128]{2,1,0:T(4,128)(2,1)} %reshape_squeeze.8), kind=kLoop, calls=%fused_computation.58 | loop fusion | flops 4186112 | bytes 4227072
  111.4 128.2 %while.10 = (s32[]{:T(128)}, f32[8,256,4,128]{3,1,2,0:T(8,128)}, s32[8]{0:T(128)}, s32[2048]{0:T(1024)}, bf16[2048,4,128]{2,1,0:T(4,128)(2,1)}, /*index=5*/s32[2...) while((s32[]{:T(128)}, f32[8,256,4,128]{3,1,2,0:T(8,128)}, ...), condition=%wide.region_11.12_spmd, body=%wide.region_4.11_spmd.sunk | while | flops 544606720 | bytes 11018043 | solution.py:83
  116.5 3.9 %conditional.4 = (f32[256,4,128]{2,0,1:T(8,128)S(1)}) conditional(s32[]{:T(128)} %convert_element_type.220, () %tuple.61, (s32[2]{0:T(128)}, s32[256]{0:T(256)S(1)}, bf16[2,512,512]{1,2,0:T(8,128)(2,1)S(1)}, bf16[256,4,128]{2,0,1:T(8,128)(2,1)S(1)}, bf16[2,512,512]{1,2,0:T(8,128)(2,1)S(1)}) %tuple.62), branch_computations={%region_7.7_spmd, %region_8.8_spmd} | conditional | flops 272237312 | bytes 4196876 | solution.py:80
  121.1 5.4 %conditional.5 = (f32[1,256,4,128]{3,1,2,0:T(8,128)S(1)}) conditional(s32[]{:T(128)} %convert_element_type.219, f32[256,4,128]{2,0,1:T(8,128)S(1)} %get-tuple-element.263, (s32[2]{0:T(128)}, s32[256]{0:T(256)S(1)}, bf16[2,512,512]{1,2,0:T(8,128)(2,1)S(1)}, bf16[256,4,128]{2,0,1:T(8,128)(2,1)S(1)}, bf16[2,512,512]{1,2,0:T(8,128)(2,1)S(1)}, ...), branch_computations={%region_9.9_spmd, %region_10.10_spmd} | conditional | flops 272368384 | bytes 4721172 | solution.py:80
  132.5 3.9 %conditional.4 = (f32[256,4,128]{2,0,1:T(8,128)S(1)}) conditional(s32[]{:T(128)} %convert_element_type.220, () %tuple.61, (s32[2]{0:T(128)}, s32[256]{0:T(256)S(1)}, bf16[2,512,512]{1,2,0:T(8,128)(2,1)S(1)}, bf16[256,4,128]{2,0,1:T(8,128)(2,1)S(1)}, bf16[2,512,512]{1,2,0:T(8,128)(2,1)S(1)}) %tuple.62), branch_computations={%region_7.7_spmd, %region_8.8_spmd} | conditional | flops 272237312 | bytes 4196876 | solution.py:80
  137.1 5.4 %conditional.5 = (f32[1,256,4,128]{3,1,2,0:T(8,128)S(1)}) conditional(s32[]{:T(128)} %convert_element_type.219, f32[256,4,128]{2,0,1:T(8,128)S(1)} %get-tuple-element.263, (s32[2]{0:T(128)}, s32[256]{0:T(256)S(1)}, bf16[2,512,512]{1,2,0:T(8,128)(2,1)S(1)}, bf16[256,4,128]{2,0,1:T(8,128)(2,1)S(1)}, bf16[2,512,512]{1,2,0:T(8,128)(2,1)S(1)}, ...), branch_computations={%region_9.9_spmd, %region_10.10_spmd} | conditional | flops 272368384 | bytes 4721172 | solution.py:80
  148.6 3.9 %conditional.4 = (f32[256,4,128]{2,0,1:T(8,128)S(1)}) conditional(s32[]{:T(128)} %convert_element_type.220, () %tuple.61, (s32[2]{0:T(128)}, s32[256]{0:T(256)S(1)}, bf16[2,512,512]{1,2,0:T(8,128)(2,1)S(1)}, bf16[256,4,128]{2,0,1:T(8,128)(2,1)S(1)}, bf16[2,512,512]{1,2,0:T(8,128)(2,1)S(1)}) %tuple.62), branch_computations={%region_7.7_spmd, %region_8.8_spmd} | conditional | flops 272237312 | bytes 4196876 | solution.py:80
  153.2 5.4 %conditional.5 = (f32[1,256,4,128]{3,1,2,0:T(8,128)S(1)}) conditional(s32[]{:T(128)} %convert_element_type.219, f32[256,4,128]{2,0,1:T(8,128)S(1)} %get-tuple-element.263, (s32[2]{0:T(128)}, s32[256]{0:T(256)S(1)}, bf16[2,512,512]{1,2,0:T(8,128)(2,1)S(1)}, bf16[256,4,128]{2,0,1:T(8,128)(2,1)S(1)}, bf16[2,512,512]{1,2,0:T(8,128)(2,1)S(1)}, ...), branch_computations={%region_9.9_spmd, %region_10.10_spmd} | conditional | flops 272368384 | bytes 4721172 | solution.py:80
  169.2 5.4 %conditional.5 = (f32[1,256,4,128]{3,1,2,0:T(8,128)S(1)}) conditional(s32[]{:T(128)} %convert_element_type.219, f32[256,4,128]{2,0,1:T(8,128)S(1)} %get-tuple-element.263, (s32[2]{0:T(128)}, s32[256]{0:T(256)S(1)}, bf16[2,512,512]{1,2,0:T(8,128)(2,1)S(1)}, bf16[256,4,128]{2,0,1:T(8,128)(2,1)S(1)}, bf16[2,512,512]{1,2,0:T(8,128)(2,1)S(1)}, ...), branch_computations={%region_9.9_spmd, %region_10.10_spmd} | conditional | flops 272368384 | bytes 4721172 | solution.py:80
  180.6 3.9 %conditional.4 = (f32[256,4,128]{2,0,1:T(8,128)S(1)}) conditional(s32[]{:T(128)} %convert_element_type.220, () %tuple.61, (s32[2]{0:T(128)}, s32[256]{0:T(256)S(1)}, bf16[2,512,512]{1,2,0:T(8,128)(2,1)S(1)}, bf16[256,4,128]{2,0,1:T(8,128)(2,1)S(1)}, bf16[2,512,512]{1,2,0:T(8,128)(2,1)S(1)}) %tuple.62), branch_computations={%region_7.7_spmd, %region_8.8_spmd} | conditional | flops 272237312 | bytes 4196876 | solution.py:80
  185.2 5.4 %conditional.5 = (f32[1,256,4,128]{3,1,2,0:T(8,128)S(1)}) conditional(s32[]{:T(128)} %convert_element_type.219, f32[256,4,128]{2,0,1:T(8,128)S(1)} %get-tuple-element.263, (s32[2]{0:T(128)}, s32[256]{0:T(256)S(1)}, bf16[2,512,512]{1,2,0:T(8,128)(2,1)S(1)}, bf16[256,4,128]{2,0,1:T(8,128)(2,1)S(1)}, bf16[2,512,512]{1,2,0:T(8,128)(2,1)S(1)}, ...), branch_computations={%region_9.9_spmd, %region_10.10_spmd} | conditional | flops 272368384 | bytes 4721172 | solution.py:80
  196.6 3.9 %conditional.4 = (f32[256,4,128]{2,0,1:T(8,128)S(1)}) conditional(s32[]{:T(128)} %convert_element_type.220, () %tuple.61, (s32[2]{0:T(128)}, s32[256]{0:T(256)S(1)}, bf16[2,512,512]{1,2,0:T(8,128)(2,1)S(1)}, bf16[256,4,128]{2,0,1:T(8,128)(2,1)S(1)}, bf16[2,512,512]{1,2,0:T(8,128)(2,1)S(1)}) %tuple.62), branch_computations={%region_7.7_spmd, %region_8.8_spmd} | conditional | flops 272237312 | bytes 4196876 | solution.py:80
  201.3 5.4 %conditional.5 = (f32[1,256,4,128]{3,1,2,0:T(8,128)S(1)}) conditional(s32[]{:T(128)} %convert_element_type.219, f32[256,4,128]{2,0,1:T(8,128)S(1)} %get-tuple-element.263, (s32[2]{0:T(128)}, s32[256]{0:T(256)S(1)}, bf16[2,512,512]{1,2,0:T(8,128)(2,1)S(1)}, bf16[256,4,128]{2,0,1:T(8,128)(2,1)S(1)}, bf16[2,512,512]{1,2,0:T(8,128)(2,1)S(1)}, ...), branch_computations={%region_9.9_spmd, %region_10.10_spmd} | conditional | flops 272368384 | bytes 4721172 | solution.py:80
  217.3 5.4 %conditional.5 = (f32[1,256,4,128]{3,1,2,0:T(8,128)S(1)}) conditional(s32[]{:T(128)} %convert_element_type.219, f32[256,4,128]{2,0,1:T(8,128)S(1)} %get-tuple-element.263, (s32[2]{0:T(128)}, s32[256]{0:T(256)S(1)}, bf16[2,512,512]{1,2,0:T(8,128)(2,1)S(1)}, bf16[256,4,128]{2,0,1:T(8,128)(2,1)S(1)}, bf16[2,512,512]{1,2,0:T(8,128)(2,1)S(1)}, ...), branch_computations={%region_9.9_spmd, %region_10.10_spmd} | conditional | flops 272368384 | bytes 4721172 | solution.py:80
  228.7 3.9 %conditional.4 = (f32[256,4,128]{2,0,1:T(8,128)S(1)}) conditional(s32[]{:T(128)} %convert_element_type.220, () %tuple.61, (s32[2]{0:T(128)}, s32[256]{0:T(256)S(1)}, bf16[2,512,512]{1,2,0:T(8,128)(2,1)S(1)}, bf16[256,4,128]{2,0,1:T(8,128)(2,1)S(1)}, bf16[2,512,512]{1,2,0:T(8,128)(2,1)S(1)}) %tuple.62), branch_computations={%region_7.7_spmd, %region_8.8_spmd} | conditional | flops 272237312 | bytes 4196876 | solution.py:80
  233.3 5.4 %conditional.5 = (f32[1,256,4,128]{3,1,2,0:T(8,128)S(1)}) conditional(s32[]{:T(128)} %convert_element_type.219, f32[256,4,128]{2,0,1:T(8,128)S(1)} %get-tuple-element.263, (s32[2]{0:T(128)}, s32[256]{0:T(256)S(1)}, bf16[2,512,512]{1,2,0:T(8,128)(2,1)S(1)}, bf16[256,4,128]{2,0,1:T(8,128)(2,1)S(1)}, bf16[2,512,512]{1,2,0:T(8,128)(2,1)S(1)}, ...), branch_computations={%region_9.9_spmd, %region_10.10_spmd} | conditional | flops 272368384 | bytes 4721172 | solution.py:80
  239.6 5.3 %reshape.260 = f32[8,256,4,128]{3,2,1,0:T(4,128)} reshape(f32[2048,1,512]{2,0,1:T(8,128)} %get-tuple-element.152) | data formatting | bytes 8388608 | tf_op jit(solution)/shard_map/convert_element_type | solution.py:91
  245.3 7.0 %copy.57 = f32[8,256,4,128]{3,2,1,0:T(4,128)} copy(f32[8,256,4,128]{3,1,2,0:T(8,128)} %get-tuple-element.93) | data formatting | bytes 8388608 | tf_op jit(solution)/shard_map/while | solution.py:83
  254.7 5.3 %all-reduce = (f32[2048]{0:T(1024)S(1)}, f32[2048]{0:T(1024)S(1)}) all-reduce(f32[2048]{0:T(1024)S(1)} %bitcast.123, f32[2048]{0:T(1024)S(1)} %bitcast.122), channel_id=1, replica_groups=mesh['users'=64,'mp'=2] {'mp'}, use_global_device_ids=true, to_apply=%region_15.16 | all-reduce | flops 4096 | bytes 32768 | tf_op jit(solution)/shard_map/psum | solution.py:93
  264.1 5.5 %mul.146 = f32[64,32,512]{2,1,0:T(8,128)} reshape(f32[2048,4,128]{2,1,0:T(4,128)} %mul.145) | data formatting | bytes 8388608 | tf_op jit(solution)/shard_map/mul | solution.py:91
  269.6 5.6 %reshape.254 = f32[64,32,512]{2,1,0:T(8,128)} reshape(f32[8,256,4,128]{3,2,1,0:T(4,128)} %copy.57) | data formatting | bytes 8388608 | tf_op jit(solution)/shard_map/reshape | solution.py:84
  275.2 6.7 %fusion.36 = bf16[64,32,512]{2,1,0:T(8,128)(2,1)} fusion(bf16[64,32,512]{2,1,0:T(8,128)(2,1)S(1)} %bitcast.115, f32[64,32,512]{2,1,0:T(8,128)} %reshape.254, f32[64,32,512]{2,1,0:T(8,128)} %mul.146, f32[64,32,512]{2,1,0:T(8,128)} %bitcast.110, f32[512]{0:T(512)S(1)} %copy-done.10, f32[64,32]{1,0:T(8,128)S(1)} %mul.153, f32[64,32]{1,0:T(8,128)S(1)} %sub.43, ...), kind=kLoop, calls=%fused_computation.56 | loop fusion | flops 9437184 | bytes 16803840 | tf_op jit(solution)/shard_map/convert_element_type | solution.py:101
  281.9 12.4 %all-gather.5.cloned.1.call-done = bf16[64,32,1024]{2,1,0:T(8,128)(2,1)} async-done(((bf16[64,32,512]{2,1,0:T(8,128)(2,1)}), bf16[64,32,1024]{2,1,0:T(8,128)(2,1)}) %all-gather.5.cloned.1.call-update) | async-done | bytes 4194320 | tf_op jit(solution)/shard_map/all_gather | solution.py:105
  294.3 5.2 %add_convert_fusion = bf16[64,32,512]{2,1,0:T(8,128)(2,1)S(1)} fusion(bf16[64,32,512]{2,1,0:T(8,128)(2,1)} %all_to_all.16, bf16[64,32,1024]{2,1,0:T(8,128)(2,1)} %all-gather.5.cloned.1.call-done, bf16[1024,512]{1,0:T(8,128)(2,1)S(1)} %copy-done.12), kind=kOutput, calls=%fused_computation.66 | convolution fusion | flops 2150629376 | bytes 9437184 | tf_op jit(solution)/shard_map/abc,cd->abd/dot_general | solution.py:103
  299.6 39.2 %all_to_all.17 = bf16[64,32,512]{2,1,0:T(8,128)(2,1)S(1)} all-to-all(bf16[64,32,512]{2,1,0:T(8,128)(2,1)S(1)} %add_convert_fusion), channel_id=1, replica_groups=mesh['users'=64,'mp'=2] {'users'}, dimensions={0} | all-to-all | bytes 4194304 | tf_op jit(solution)/shard_map/all_to_all | solution.py:110
  (211 shorter events, 152.0 us)
Async XLA Ops:
  6.5 2.1 copy-start
  6.5 65.1 %all-gather.3.cloned.1.call-start = ((), (), s32[]{:S(2)}) async-start(), calls=%async_computation.3 | async-start | bytes 6291456 | tf_op jit(solution)/shard_map/all_gather | solution.py:44
  11.0 51.3 %copy-start.5 = (bf16[2,512,512]{2,1,0:T(8,128)(2,1)S(1)}, bf16[2,512,512]{2,1,0:T(8,128)(2,1)}, u32[]{:S(2)}) copy-start(bf16[2,512,512]{2,1,0:T(8,128)(2,1)} %param.20) | copy-start | bytes 3145732
  11.0 51.8 %copy-start.6 = (bf16[2,512,512]{2,1,0:T(8,128)(2,1)S(1)}, bf16[2,512,512]{2,1,0:T(8,128)(2,1)}, u32[]{:S(2)}) copy-start(bf16[2,512,512]{2,1,0:T(8,128)(2,1)} %param.21) | copy-start | bytes 3145732
  53.4 15.6 %all-to-all-start.1 = ((bf16[64,1,32]{2,1,0:T(2,128)(2,1)}), bf16[64,1,32]{2,1,0:T(2,128)(2,1)S(1)}, u32[]{:S(2)}, u32[]{:S(2)}) async-start(bf16[64,1,32]{2,1,0:T(2,128)(2,1)} %convert_element_type.173), calls=%async_computation.1 | async-start | bytes 65536 | tf_op jit(solution)/shard_map/all_to_all | solution.py:41
  60.6 233.7 %all-gather.5.cloned.1.call-start = ((), (), s32[]{:S(2)}) async-start(), calls=%async_computation.4 | async-start | bytes 6291456 | tf_op jit(solution)/shard_map/all_gather | solution.py:105
  71.7 6.0 %copy-start.9 = (f32[1024]{0:T(1024)S(1)}, f32[1024]{0:T(1024)}, u32[]{:S(2)}) copy-start(f32[1024]{0:T(1024)} %param.22) | copy-start | bytes 12292
  77.7 3.5 copy-start.11
  239.6 5.3 %copy-start.7 = (f32[2048,4]{0,1:T(4,128)S(1)}, f32[2048,4]{0,1:T(4,128)}, u32[]{:S(2)}) copy-start(f32[2048,4]{0,1:T(4,128)} %fusion.58) | copy-start | bytes 98308
  245.2 7.0 %copy-start.2 = (f32[8,256,4,128]{3,1,2,0:T(8,128)S(1)}, f32[8,256,4,128]{3,1,2,0:T(8,128)}, u32[]{:S(2)}) copy-start(f32[8,256,4,128]{3,1,2,0:T(8,128)} %get-tuple-element.93) | copy-start | bytes 12582916
  245.2 7.0 %copy-start.3 = (f32[8,256,4,128]{3,2,1,0:T(4,128)S(1)}, f32[8,256,4,128]{3,2,1,0:T(4,128)}, u32[]{:S(2)}) copy-start(f32[8,256,4,128]{3,2,1,0:T(4,128)} %reshape.260) | copy-start | bytes 12582916
  269.6 5.6 %copy-start.4 = (bf16[2048,1,512]{2,0,1:T(8,128)(2,1)S(1)}, bf16[2048,1,512]{2,0,1:T(8,128)(2,1)}, u32[]{:S(2)}) copy-start(bf16[2048,1,512]{2,0,1:T(8,128)(2,1)} %get-tuple-element.153) | copy-start | bytes 6291460
  269.6 5.6 %copy-start.8 = (f32[64,1,32]{2,1,0:T(1,128)S(1)}, f32[64,1,32]{2,1,0:T(1,128)}, u32[]{:S(2)}) copy-start(f32[64,1,32]{2,1,0:T(1,128)} %get-tuple-element.151) | copy-start | bytes 24580
  269.6 5.6 %copy-start.10 = (f32[512]{0:T(512)S(1)}, f32[512]{0:T(512)}, u32[]{:S(2)}) copy-start(f32[512]{0:T(512)} %param.24) | copy-start | bytes 6148
  275.2 19.1 %copy-start.12 = (bf16[1024,512]{1,0:T(8,128)(2,1)S(1)}, bf16[1024,512]{1,0:T(8,128)(2,1)}, u32[]{:S(2)}) copy-start(bf16[1024,512]{1,0:T(8,128)(2,1)} %param.25) | copy-start | bytes 3145732
  338.8 3.4 copy-start.1
Sparse Core Ops, SparseCore 0:
  51.6 15.3 all-gather.2
  282.0 12.2 all-gather.4
where the time goes:
time: 352 us; the launch traced here: 349 us
  local copies, waits for them, and re-layouts  91.5 us (26%)
  blocking collectives  85 us (24%)
  matrix products  60.3 us (17%)
  other arithmetic  55.9 us (16%)
  loops' own time  17 us (5%)
  waiting for transfers between devices  16.7 us (5%)
  between operations  15 us (4%)
  starting transfers between devices  7.46 us (2%)
    all_to_all x1, blocking collectives, body(): lax.all_to_all(buffer, 'users', split_axis=0, concat_axis=0, tiled=True)  40.5 us
    all_to_all x1, blocking collectives, body(): lax.all_to_all(finished, 'users', split_axis=0, concat_axis=0, tiled=True)  39.2 us
    dot_general x16, matrix products, attend(): jnp.einsum('rhp,phc->rhc', wts, vals, preferred_element_type=jnp.float32)  36.5 us
    another operation x1, loops' own time, body(): blocks_out = lax.map(one_block, jnp.arange(total // block, dtype=jnp.int32))  16.3 us
    slice x16, local copies, waits for them, and re-layouts, attend(): vals = v_cache[user].reshape(HLEN, heads_here, HD)  13.2 us
    all_gather x1, waiting for transfers between devices, body(): lax.all_gather(y_rows, 'mp', axis=2, tiled=True)  12.4 us
    reduce_or x8, other arithmetic, one_block(): touches = jnp.any(key_b == user)  11.8 us
    dot_general x1, matrix products, body(): jnp.einsum('rd,dgc->rgc', normed, w_uvqk, preferred_element_type=jnp.floa...  11.6 us
  transfers between devices with their start and end apart: 3, of which 2 were waited for; matrix products, arithmetic and copies ran while one was open for 2% of the time, Pallas kernels for 0%

commit v1 on v0

v1 whole, which is shorter than its diff:
```python
import functools
import math

import jax
import jax.numpy as jnp
from jax import lax
from jax.experimental import pallas as pl
from jax.experimental.pallas import tpu as pltpu
from jax.sharding import PartitionSpec as P

MESH = pl.DeviceIdType.MESH
D = 1024
W = 512
HD = 128
HEADS_HERE = W // HD
HLEN = 512
ROWS = 1024
PEERS = 64
SIDE = 4
CAP = 32
SLOTS = PEERS * CAP
GROUP = 8
GROUPS = PEERS // GROUP
GR = GROUP * CAP
STEP = 59
STEP_INV = 51
LAG = 4
EPS = 1e-05
SCALE = 1.0 / math.sqrt(HD)
F32 = jnp.float32
BF16 = jnp.bfloat16


def silu(x):
    t = 0.5 * x
    return t + t * jnp.tanh(t)


def digits(k):
    return k % SIDE, (k // SIDE) % SIDE, k // (SIDE * SIDE)


def ahead(me, j):
    x, y, z = digits(me)
    a, b, c = digits((j * STEP) % PEERS)
    return ((z + c) % SIDE) * SIDE * SIDE + ((y + b) % SIDE) * SIDE + (x + a) % SIDE


def behind(me, j):
    x, y, z = digits(me)
    a, b, c = digits((j * STEP) % PEERS)
    return (
        ((z + SIDE - c) % SIDE) * SIDE * SIDE
        + ((y + SIDE - b) % SIDE) * SIDE
        + (x + SIDE - a) % SIDE
    )


def mirrored(j):
    a, b, c = digits((j * STEP) % PEERS)
    k = ((SIDE - c) % SIDE) * SIDE * SIDE + ((SIDE - b) % SIDE) * SIDE + (SIDE - a) % SIDE
    return (k * STEP_INV) % PEERS


def kernel(
    x_hbm, dest_ref, slot_ref, hist_ref, k_hbm, v_hbm, in_gain_ref, w_hbm, attn_gain_ref, wout_hbm,
    out_ref,
    x_v, w_v, wout_v, k_v, v_v, v01, fs_row, fs_col, meta, metar, mask_in, inv_len, gain_v,
    xs_own, xs_peer, h_v, q_send, q_recv, a_send, back, u_v, self_v, st_send, st_recv,
    y_own, y_peer, acc,
    load_sem, x_ssem, x_rsem, q_ssem, q_rsem, a_ssem, a_rsem, m_ssem, m_rsem, s_ssem, s_rsem,
    y_ssem, y_rsem,
):
    me = lax.axis_index("users")
    mp = lax.axis_index("mp")
    other = 1 - mp
    own_at = pl.multiple_of(mp * W, W)
    peer_at = pl.multiple_of(other * W, W)

    loads = [
        pltpu.make_async_copy(x_hbm, x_v, load_sem.at[0]),
        pltpu.make_async_copy(w_hbm.at[2, pl.ds(own_at, W)], w_v.at[2, pl.ds(0, W)], load_sem.at[1]),
        pltpu.make_async_copy(w_hbm.at[2, pl.ds(peer_at, W)], w_v.at[2, pl.ds(W, W)], load_sem.at[2]),
        pltpu.make_async_copy(k_hbm, k_v, load_sem.at[3]),
        pltpu.make_async_copy(v_hbm, v_v, load_sem.at[4]),
    ]
    late = [
        pltpu.make_async_copy(wout_hbm.at[pl.ds(own_at, W)], wout_v.at[pl.ds(0, W)], load_sem.at[5]),
        pltpu.make_async_copy(wout_hbm.at[pl.ds(peer_at, W)], wout_v.at[pl.ds(W, W)], load_sem.at[6]),
    ]
    for n, g in enumerate((0, 1, 3)):
        late.append(
            pltpu.make_async_copy(
                w_hbm.at[g, pl.ds(own_at, W)], w_v.at[g, pl.ds(0, W)], load_sem.at[7 + 2 * n]
            )
        )
        late.append(
            pltpu.make_async_copy(
                w_hbm.at[g, pl.ds(peer_at, W)], w_v.at[g, pl.ds(W, W)], load_sem.at[8 + 2 * n]
            )
        )
    for c in loads + late:
        c.start()

    barrier = pltpu.get_barrier_semaphore()

    def greet(j, carry):
        pl.semaphore_signal(barrier, inc=1, device_id=(ahead(me, j), mp), device_id_type=MESH)
        return carry

    pl.semaphore_signal(barrier, inc=1, device_id=(me, other), device_id_type=MESH)
    lax.fori_loop(1, PEERS, greet, 0)

    dest = dest_ref[...]
    slot = slot_ref[...]
    mx, my, mz = digits(me)
    kx = ((dest & 3) + (SIDE - mx)) & 3
    ky = (((dest >> 2) & 3) + (SIDE - my)) & 3
    kz = ((dest >> 4) + (SIDE - mz)) & 3
    number = ((kx + 4 * ky + 16 * kz) * STEP_INV) & (PEERS - 1)
    key = 2 * number + slot
    hot = (lax.broadcasted_iota(jnp.int32, (2 * PEERS, ROWS), 0) == key).astype(F32)
    before = jnp.zeros((2 * PEERS, 256), F32)
    pos_parts = []
    tri = (
        lax.broadcasted_iota(jnp.int32, (256, 256), 0)
        < lax.broadcasted_iota(jnp.int32, (256, 256), 1)
    ).astype(F32).astype(BF16)
    count = jnp.zeros((2 * PEERS, 1), F32)
    for b in range(ROWS // 256):
        part = hot[:, b * 256 : (b + 1) * 256]
        before = jnp.dot(part.astype(BF16), tri, preferred_element_type=F32) + count
        pos_parts.append(jnp.sum(before * part, axis=0, keepdims=True))
        count = count + jnp.sum(part, axis=1, keepdims=True)
    pos = jnp.concatenate(pos_parts, axis=1)
    fs = (number * CAP).astype(F32) + jnp.where(slot == 0, pos, (CAP - 1) - pos)
    fs_row[...] = jnp.broadcast_to(fs, (8, ROWS))
    fs_col[...] = jnp.broadcast_to(fs, (HD, ROWS)).T
    same = lax.broadcasted_iota(jnp.int32, (PEERS, ROWS), 0) == number
    first = jnp.sum(jnp.where(same & (slot == 0), 1.0, 0.0), axis=1, keepdims=True)
    hist = hist_ref[...].astype(F32)
    len0, len1 = hist[:, 0:1], hist[:, 1:2]
    lane = lax.broadcasted_iota(jnp.int32, (PEERS, HD), 1)
    meta_rows = jnp.where(lane < 64, first, jnp.where(lane < 96, len0, len1))
    meta[...] = meta_rows.reshape(PEERS, 1, HD)
    metar[0] = meta[0]
    gain_v[...] = jnp.concatenate(
        [in_gain_ref[pl.ds(mp, 1), :], in_gain_ref[pl.ds(other, 1), :]], axis=1
    )
    acc[...] = jnp.zeros_like(acc)

    def rows_of(g):
        return pl.ds(pl.multiple_of(g * GR, GR), GR)

    def chunk_of(j):
        return pl.ds(pl.multiple_of(j * CAP, CAP), CAP)

    def x_copy(g):
        return pltpu.make_async_remote_copy(
            src_ref=xs_own.at[rows_of(g)], dst_ref=xs_peer.at[rows_of(g)],
            send_sem=x_ssem.at[g], recv_sem=x_rsem.at[g],
            device_id=(me, other), device_id_type=MESH,
        )

    def q_copy(g, j):
        return pltpu.make_async_remote_copy(
            src_ref=q_send.at[chunk_of(j)], dst_ref=q_recv.at[chunk_of(j)],
            send_sem=q_ssem.at[g], recv_sem=q_rsem.at[g],
            device_id=(ahead(me, j), mp), device_id_type=MESH,
        )

    def a_copy(g, j):
        return pltpu.make_async_remote_copy(
            src_ref=a_send.at[chunk_of(j)], dst_ref=back.at[chunk_of(j)],
            send_sem=a_ssem.at[g], recv_sem=a_rsem.at[g],
            device_id=(behind(me, j), mp), device_id_type=MESH,
        )

    def s_copy(g):
        return pltpu.make_async_remote_copy(
            src_ref=st_send.at[rows_of(g)], dst_ref=st_recv.at[rows_of(g)],
            send_sem=s_ssem.at[g], recv_sem=s_rsem.at[g],
            device_id=(me, other), device_id_type=MESH,
        )

    def y_copy(g):
        return pltpu.make_async_remote_copy(
            src_ref=y_own.at[rows_of(g)], dst_ref=y_peer.at[rows_of(g)],
            send_sem=y_ssem.at[g], recv_sem=y_rsem.at[g],
            device_id=(me, other), device_id_type=MESH,
        )

    def m_copy(j):
        return pltpu.make_async_remote_copy(
            src_ref=meta.at[j], dst_ref=metar.at[j],
            send_sem=m_ssem.at[0], recv_sem=m_rsem.at[0],
            device_id=(ahead(me, j), mp), device_id_type=MESH,
        )

    def gather(g):
        slots = lax.broadcasted_iota(jnp.int32, (GR, ROWS), 0).astype(F32) + (g * GR).astype(F32)
        pick = jnp.where(slots == fs_row[0:1, :], 1.0, 0.0).astype(BF16)
        xs_own[rows_of(g), :] = jnp.dot(pick, x_v[...], preferred_element_type=F32).astype(BF16)
        x_copy(g).start()

    def norm_and_query(g):
        x_copy(g).wait_recv()
        xo = xs_own[rows_of(g), :].astype(F32)
        xp = xs_peer[rows_of(g), :].astype(F32)
        xf = jnp.concatenate([xo, xp], axis=1)
        mean = jnp.sum(xf, axis=1, keepdims=True) * (1.0 / D)
        c = xf - mean
        var = jnp.sum(c * c, axis=1, keepdims=True) * (1.0 / D)
        h = (c * lax.rsqrt(var + EPS) * gain_v[...]).astype(BF16)
        h_v[rows_of(g), :] = h
        q_send[rows_of(g), :] = silu(jnp.dot(h, w_v[2], preferred_element_type=F32)).astype(BF16)

    def send_queries(g):
        lo = jnp.where(g == 0, 1, g * GROUP)

        def one(j, carry):
            q_copy(g, j).start()
            return carry

        lax.fori_loop(lo, (g + 1) * GROUP, one, 0)

    def project_rest(g):
        h = h_v[rows_of(g), :]
        u_v[rows_of(g), :] = silu(jnp.dot(h, w_v[0], preferred_element_type=F32)).astype(BF16)
        v = silu(jnp.dot(h, w_v[1], preferred_element_type=F32)).astype(BF16).astype(F32)
        k = silu(jnp.dot(h, w_v[3], preferred_element_type=F32)).astype(BF16).astype(F32)
        q = q_send[rows_of(g), :].astype(F32)
        qk = q * k
        for n in range(HEADS_HERE):
            cols = slice(n * HD, (n + 1) * HD)
            s = jnp.sum(qk[:, cols], axis=1, keepdims=True) * SCALE
            sw = silu(s).astype(BF16).astype(F32)
            self_v[rows_of(g), cols] = sw * v[:, cols] * inv_len[rows_of(g), :]

    def attend(g):
        m1 = mask_in[rows_of(g), :]
        m0 = 1.0 - m1
        rs = m0 * (1.0 / (len0 + 1.0)) + m1 * (1.0 / (len1 + 1.0))
        for n in range(HEADS_HERE):
            cols = slice(n * HD, (n + 1) * HD)
            qf = q_recv[rows_of(g), cols].astype(F32)
            q01 = jnp.concatenate([(qf * m0).astype(BF16), (qf * m1).astype(BF16)], axis=1)
            k01 = jnp.concatenate([k_v[0, :, cols], k_v[1, :, cols]], axis=1)
            s = lax.dot_general(q01, k01, (((1,), (1,)), ((), ())), preferred_element_type=F32)
            t = s * (0.5 * SCALE)
            wts = (t + t * jnp.tanh(t)).astype(BF16)
            o = jnp.dot(wts, v01[n], preferred_element_type=F32)
            a = (o[:, :HD] * m0 + o[:, HD:] * m1) * rs
            a_send[rows_of(g), cols] = a.astype(BF16)

    def send_back(g):
        lo = jnp.where(g == 0, 1, g * GROUP)

        def one(j, carry):
            a_copy(g, j).start()
            return carry

        lax.fori_loop(lo, (g + 1) * GROUP, one, 0)

    def finish_sums(g):
        a = back[rows_of(g), :].astype(F32) + self_v[rows_of(g), :]
        mean = jnp.sum(a, axis=1, keepdims=True) * (1.0 / W)
        c = a - mean
        m2 = jnp.sum(c * c, axis=1, keepdims=True)
        self_v[rows_of(g), :] = a
        lanes = lax.broadcasted_iota(jnp.int32, (GR, HD), 1)
        st_send[rows_of(g), :] = jnp.where(lanes < 64, mean, m2)
        s_copy(g).start()

    def normalize(g):
        s_copy(g).wait_recv()
        so = st_send[rows_of(g), :]
        sp = st_recv[rows_of(g), :]
        mo, mp_ = so[:, 0:1], sp[:, 0:1]
        mean = 0.5 * (mo + mp_)
        gap = mo - mp_
        var = (so[:, 64:65] + sp[:, 64:65] + (0.5 * W) * gap * gap) * (1.0 / D)
        y = (
            (self_v[rows_of(g), :] - mean)
            * lax.rsqrt(var + EPS)
            * attn_gain_ref[...]
            * u_v[rows_of(g), :].astype(F32)
        )
        y_own[rows_of(g), :] = y.astype(BF16)
        y_copy(g).start()

    def output(g):
        y_copy(g).wait_recv()
        y = jnp.concatenate([y_own[rows_of(g), :], y_peer[rows_of(g), :]], axis=1)
        p = jnp.dot(y, wout_v[...], preferred_element_type=F32)
        fin = (xs_own[rows_of(g), :].astype(F32) + p).astype(BF16)
        base = (g * GR).astype(F32)
        lanes = lax.broadcasted_iota(jnp.int32, (ROWS, HD), 1).astype(F32) + base
        f = fs_col[...]
        pick = jnp.concatenate(
            [jnp.where(f == lanes + float(n * HD), 1.0, 0.0).astype(BF16) for n in range(GR // HD)],
            axis=1,
        )
        acc[...] += jnp.dot(pick, fin, preferred_element_type=F32)

    pl.semaphore_wait(barrier, PEERS)

    def send_meta(j, carry):
        m_copy(j).start()
        return carry

    lax.fori_loop(1, PEERS, send_meta, 0)
    for c in loads[:3]:
        c.wait()

    def head(i, carry):
        @pl.when(i < GROUPS)
        def _():
            gather(i)

        @pl.when(i >= 1)
        def _():
            norm_and_query(i - 1)

            @pl.when(i == 1)
            def _():
                q_recv[pl.ds(0, CAP), :] = q_send[pl.ds(0, CAP), :]

            send_queries(i - 1)

        return carry

    lax.fori_loop(0, GROUPS + 1, head, 0)

    for c in loads[3:] + late:
        c.wait()
    place = lax.broadcasted_iota(jnp.int32, (HLEN, W), 0).astype(F32)
    for user, length in ((0, len0), (1, len1)):
        kept = jnp.where(place < length, v_v[user].astype(F32), 0.0).astype(BF16)
        for n in range(HEADS_HERE):
            v01[n, :, user * HD : (user + 1) * HD] = kept[:, n * HD : (n + 1) * HD]

    pltpu.make_async_copy(
        metar.at[pl.ds(1, PEERS - 1)], metar.at[pl.ds(1, PEERS - 1)], m_rsem.at[0]
    ).wait()
    in_chunk = lax.broadcasted_iota(jnp.int32, (CAP, HD), 0).astype(F32)

    def masks(j, carry):
        mask_in[chunk_of(j), :] = jnp.where(in_chunk >= metar[j][:, 0:1], 1.0, 0.0)
        theirs = metar[mirrored(j)]
        l0, l1 = theirs[:, 64:65], theirs[:, 96:97]
        length = jnp.where(in_chunk >= meta[j][:, 0:1], l1, l0)
        inv_len[chunk_of(j), :] = 1.0 / (length + 1.0)
        return carry

    lax.fori_loop(0, PEERS, masks, 0)

    def wait_group(buf, sem, g):
        @pl.when(g == 0)
        def _():
            rows = pl.ds(CAP, GR - CAP)
            pltpu.make_async_copy(buf.at[rows], buf.at[rows], sem.at[0]).wait()

        @pl.when(g > 0)
        def _():
            pltpu.make_async_copy(buf.at[rows_of(g)], buf.at[rows_of(g)], sem.at[g]).wait()

    def body(i, carry):
        @pl.when(i < GROUPS)
        def _():
            project_rest(i)
            wait_group(q_recv, q_rsem, i)
            attend(i)

            @pl.when(i == 0)
            def _():
                back[pl.ds(0, CAP), :] = a_send[pl.ds(0, CAP), :]

            send_back(i)

        @pl.when(jnp.logical_and(i >= LAG, i < GROUPS + LAG))
        def _():
            wait_group(back, a_rsem, i - LAG)
            finish_sums(i - LAG)

        @pl.when(jnp.logical_and(i >= LAG + 1, i < GROUPS + LAG + 1))
        def _():
            normalize(i - LAG - 1)

        @pl.when(i >= LAG + 2)
        def _():
            output(i - LAG - 2)

        return carry

    lax.fori_loop(0, GROUPS + LAG + 2, body, 0)
    out_ref[...] = acc[...].astype(BF16)

    def drain(g, carry):
        x_copy(g).wait_send()
        s_copy(g).wait_send()
        y_copy(g).wait_send()
        wait_group(q_send, q_ssem, g)
        wait_group(a_send, a_ssem, g)
        return carry

    lax.fori_loop(0, GROUPS, drain, 0)
    pltpu.make_async_copy(
        meta.at[pl.ds(1, PEERS - 1)], meta.at[pl.ds(1, PEERS - 1)], m_ssem.at[0]
    ).wait()


def body(
    candidates, cand_dest, cand_slot, hist_len, k_cache, v_cache, in_gain, w_uvqk, attn_gain, w_out
):
    vmem = pl.BlockSpec(memory_space=pltpu.VMEM)
    hbm = pl.BlockSpec(memory_space=pl.ANY)
    dma = pltpu.SemaphoreType.DMA
    return pl.pallas_call(
        kernel,
        out_shape=jax.ShapeDtypeStruct((ROWS, W), BF16),
        in_specs=[hbm, vmem, vmem, vmem, hbm, hbm, vmem, hbm, vmem, hbm],
        out_specs=vmem,
        scratch_shapes=[
            pltpu.VMEM((ROWS, W), BF16),
            pltpu.VMEM((4, D, W), BF16),
            pltpu.VMEM((D, W), BF16),
            pltpu.VMEM((2, HLEN, W), BF16),
            pltpu.VMEM((2, HLEN, W), BF16),
            pltpu.VMEM((HEADS_HERE, HLEN, 2 * HD), BF16),
            pltpu.VMEM((8, ROWS), F32),
            pltpu.VMEM((ROWS, HD), F32),
            pltpu.VMEM((PEERS, 1, HD), F32),
            pltpu.VMEM((PEERS, 1, HD), F32),
            pltpu.VMEM((SLOTS, HD), F32),
            pltpu.VMEM((SLOTS, HD), F32),
            pltpu.VMEM((1, D), F32),
            pltpu.VMEM((SLOTS, W), BF16),
            pltpu.VMEM((SLOTS, W), BF16),
            pltpu.VMEM((SLOTS, D), BF16),
            pltpu.VMEM((SLOTS, W), BF16),
            pltpu.VMEM((SLOTS, W), BF16),
            pltpu.VMEM((SLOTS, W), BF16),
            pltpu.VMEM((SLOTS, W), BF16),
            pltpu.VMEM((SLOTS, W), BF16),
            pltpu.VMEM((SLOTS, W), F32),
            pltpu.VMEM((SLOTS, HD), F32),
            pltpu.VMEM((SLOTS, HD), F32),
            pltpu.VMEM((SLOTS, W), BF16),
            pltpu.VMEM((SLOTS, W), BF16),
            pltpu.VMEM((ROWS, W), F32),
            dma((13,)),
            dma((GROUPS,)), dma((GROUPS,)),
            dma((GROUPS,)), dma((GROUPS,)),
            dma((GROUPS,)), dma((GROUPS,)),
            dma((1,)), dma((1,)),
            dma((GROUPS,)), dma((GROUPS,)),
            dma((GROUPS,)), dma((GROUPS,)),
        ],
        compiler_params=pltpu.CompilerParams(
            collective_id=0, has_side_effects=True, vmem_limit_bytes=60 * 2**20
        ),
        cost_estimate=pl.CostEstimate(
            flops=20 * 10**9, bytes_accessed=10 * 10**6, transcendentals=9 * 10**6
        ),
        name="routed_ranking",
    )(
        candidates,
        cand_dest.reshape(1, ROWS),
        cand_slot.reshape(1, ROWS),
        hist_len,
        k_cache,
        v_cache,
        in_gain.reshape(2, W),
        w_uvqk.transpose(1, 0, 2),
        attn_gain.reshape(1, W),
        w_out,
    )


def solution(mesh):
    return jax.shard_map(
        body,
        mesh=mesh,
        in_specs=(
            P("users", "mp"),
            P("users", None),
            P("users"),
            P("users", None),
            P("users", None, "mp"),
            P("users", None, "mp"),
            P(),
            P(None, None, "mp"),
            P("mp"),
            P(None, "mp"),
        ),
        out_specs=P("users", "mp"),
        check_vma=False,
    )
```

time: 352 us -> 93.3 us (0.27)
  blocking collectives: 85 us -> 0 us
  Pallas kernels: 0 us -> 84.6 us
  local copies, waits for them, and re-layouts: 91.5 us -> 8.5 us
  matrix products: 60.3 us -> 0 us
  other arithmetic: 55.9 us -> 0 us
  loops' own time: 17 us -> 0 us
  waiting for transfers between devices: 16.7 us -> 0 us
  between operations: 15 us -> 0.01 us
  starting transfers between devices: 7.46 us -> 0 us
    pallas_call x0 -> x1, Pallas kernels: none -> 84.6 us  [body(): pl.pallas_call(kernel, out_shape=jax.ShapeDtypeStruct((ROWS, W), BF16), i...]
    all_to_all x2 -> x0, blocking collectives: 79.7 us -> none  [the longest x1 40.5 us: body(): lax.all_to_all(buffer, 'users', split_axis=0, concat_axis=0, tiled=True)]
    dot_general x21 -> x0, matrix products: 60.3 us -> none  [the longest x16 36.5 us: attend(): jnp.einsum('rhp,phc->rhc', wts, vals, preferred_element_type=jnp.float32)]
    slice x41 -> x0, local copies, waits for them, and re-layouts: 25.8 us -> none  [the longest x16 13.2 us: attend(): vals = v_cache[user].reshape(HLEN, heads_here, HD)]
    dynamic_slice x24 -> x0, local copies, waits for them, and re-layouts: 18.8 us -> none  [the longest x8 10.1 us: body(): blocks_out = lax.map(one_block, jnp.arange(total // block, dtype=jnp.int32))]
    another operation x17 -> x0, loops' own time: 17 us -> none  [the longest x1 16.3 us: body(): blocks_out = lax.map(one_block, jnp.arange(total // block, dtype=jnp.int32))]
    convert_element_type x7 -> x0, other arithmetic: 15.4 us -> none  [the longest x1 6.65 us: body(): y_rows = ((attn - mean_at[:, None]) * lax.rsqrt(var_at[:, None] + 1e-05)...]
    all_gather x2 -> x0, waiting for transfers between devices: 12.4 us -> none  [the longest x1 12.4 us: body(): lax.all_gather(y_rows, 'mp', axis=2, tiled=True)]
  transfers between devices with their start and end apart: 3 -> 0, of which waited for: 2 -> 0; matrix products, arithmetic and copies ran while one was open for 2% -> 0% of each run, Pallas kernels for 0% -> 0%
where the time goes in v1:
time: 93.3 us; the launch traced here: 93.1 us
  Pallas kernels  84.6 us (91%)
  local copies, waits for them, and re-layouts  8.5 us (9%)
    pallas_call x1, Pallas kernels, body(): pl.pallas_call(kernel, out_shape=jax.ShapeDtypeStruct((ROWS, W), BF16), i...  84.6 us
    unnamed x2, local copies, waits for them, and re-layouts  7.21 us

profile of v1, /device:TPU:1, one launch (start us, length us, event | category | flops | bytes accessed | tf_op | source)
XLA Modules:
  0.0 93.1 jit_solution(3784153891644062545)
XLA Ops:
  0.0 1.3 %reshape.14.in_gain_ref = f32[2,512]{1,0:T(2,128)} reshape(f32[1024]{0:T(1024)} %param.16) | data formatting | bytes 8192 | tf_op jit(solution)/shard_map/reshape | solution.py:474
  1.3 4.9 %copy.13 = bf16[1024,4,512]{2,0,1:T(8,128)(2,1)} copy(bf16[1024,4,512]{2,1,0:T(4,128)(2,1)} %param.17) | data formatting | bytes 8388608 | tf_op args[7]
  6.2 84.6 %routed_ranking.1 = bf16[1024,512]{1,0:T(8,128)(2,1)} custom-call(bf16[1024,512]{1,0:T(8,128)(2,1)} %x_hbm.1, s32[1,1024]{1,0:T(1,128)} %bitcast.7, s32[1,1024]{1,0:T(1,128)} %bitcast.8, s32[1,2]{1,0:T(1,128)} %hist_ref.1, bf16[2,512,512]{2,1,0:T(8,128)(2,1)} %k_hbm.1, bf16[2,512,512]{2,1,0:T(8,128)(2,1)} %v_hbm.1, f32[2,512]{1,0:T(2,128)} %reshape.14.in_gain_ref, ...), custom_call_target="tpu_custom_call" | custom-call | flops 20000000000 | bytes 10000000 | tf_op jit(solution)/shard_map/routed_ranking/pallas_call | solution.py:419
  90.8 2.3 %copy.15 = bf16[1024,512]{1,0:T(8,128)(2,1)} copy(bf16[1024,512]{1,0:T(8,128)(2,1)} %routed_ranking.1) | data formatting | bytes 2097152

commit v2 on v1

--- a/solution.py
+++ b/solution.py
@@ -26,6 +26,8 @@
 STEP_INV = 51
 LAG = 4
 EPS = 1e-05
+VMEM_LIMIT = 54 * 2**20
+ABL = CAP
 SCALE = 1.0 / math.sqrt(HD)
 F32 = jnp.float32
 BF16 = jnp.bfloat16
@@ -65,7 +67,7 @@
 def kernel(
     x_hbm, dest_ref, slot_ref, hist_ref, k_hbm, v_hbm, in_gain_ref, w_hbm, attn_gain_ref, wout_hbm,
     out_ref,
-    x_v, w_v, wout_v, k_v, v_v, v01, fs_row, fs_col, meta, metar, mask_in, inv_len, gain_v,
+    x_v, w_raw, w_v, wout_v, k_v, v_v, v01, fs_row, fs_col, meta, metar, mask_in, inv_len, gain_v,
     xs_own, xs_peer, h_v, q_send, q_recv, a_send, back, u_v, self_v, st_send, st_recv,
     y_own, y_peer, acc,
     load_sem, x_ssem, x_rsem, q_ssem, q_rsem, a_ssem, a_rsem, m_ssem, m_rsem, s_ssem, s_rsem,
@@ -77,39 +79,27 @@
     own_at = pl.multiple_of(mp * W, W)
     peer_at = pl.multiple_of(other * W, W)
 
+    barrier = pltpu.get_barrier_semaphore()
+
+    def greet(j, carry):
+        pl.semaphore_signal(barrier, inc=1, device_id=(ahead(me, j), mp), device_id_type=MESH)
+        return carry
+
+    pl.semaphore_signal(barrier, inc=1, device_id=(me, other), device_id_type=MESH)
+    lax.fori_loop(1, PEERS, greet, 0)
+
     loads = [
         pltpu.make_async_copy(x_hbm, x_v, load_sem.at[0]),
-        pltpu.make_async_copy(w_hbm.at[2, pl.ds(own_at, W)], w_v.at[2, pl.ds(0, W)], load_sem.at[1]),
-        pltpu.make_async_copy(w_hbm.at[2, pl.ds(peer_at, W)], w_v.at[2, pl.ds(W, W)], load_sem.at[2]),
+        pltpu.make_async_copy(w_hbm, w_raw, load_sem.at[1]),
+        pltpu.make_async_copy(wout_hbm.at[pl.ds(own_at, W)], wout_v.at[pl.ds(0, W)], load_sem.at[2]),
         pltpu.make_async_copy(k_hbm, k_v, load_sem.at[3]),
         pltpu.make_async_copy(v_hbm, v_v, load_sem.at[4]),
     ]
-    late = [
-        pltpu.make_async_copy(wout_hbm.at[pl.ds(own_at, W)], wout_v.at[pl.ds(0, W)], load_sem.at[5]),
-        pltpu.make_async_copy(wout_hbm.at[pl.ds(peer_at, W)], wout_v.at[pl.ds(W, W)], load_sem.at[6]),
-    ]
-    for n, g in enumerate((0, 1, 3)):
-        late.append(
-            pltpu.make_async_copy(
-                w_hbm.at[g, pl.ds(own_at, W)], w_v.at[g, pl.ds(0, W)], load_sem.at[7 + 2 * n]
-            )
-        )
-        late.append(
-            pltpu.make_async_copy(
-                w_hbm.at[g, pl.ds(peer_at, W)], w_v.at[g, pl.ds(W, W)], load_sem.at[8 + 2 * n]
-            )
-        )
-    for c in loads + late:
+    loads.append(
+        pltpu.make_async_copy(wout_hbm.at[pl.ds(peer_at, W)], wout_v.at[pl.ds(W, W)], load_sem.at[5])
+    )
+    for c in loads:
         c.start()
-
-    barrier = pltpu.get_barrier_semaphore()
-
-    def greet(j, carry):
-        pl.semaphore_signal(barrier, inc=1, device_id=(ahead(me, j), mp), device_id_type=MESH)
-        return carry
-
-    pl.semaphore_signal(barrier, inc=1, device_id=(me, other), device_id_type=MESH)
-    lax.fori_loop(1, PEERS, greet, 0)
 
     dest = dest_ref[...]
     slot = slot_ref[...]
@@ -145,7 +135,7 @@
     meta[...] = meta_rows.reshape(PEERS, 1, HD)
     metar[0] = meta[0]
     gain_v[...] = jnp.concatenate(
-        [in_gain_ref[pl.ds(mp, 1), :], in_gain_ref[pl.ds(other, 1), :]], axis=1
+        [in_gain_ref[:, pl.ds(own_at, W)], in_gain_ref[:, pl.ds(peer_at, W)]], axis=1
     )
     acc[...] = jnp.zeros_like(acc)
 
@@ -154,6 +144,9 @@
 
     def chunk_of(j):
         return pl.ds(pl.multiple_of(j * CAP, CAP), CAP)
+
+    def abl_of(j):
+        return pl.ds(pl.multiple_of(j * CAP, CAP), ABL)
 
     def x_copy(g):
         return pltpu.make_async_remote_copy(
@@ -164,14 +157,14 @@
 
     def q_copy(g, j):
         return pltpu.make_async_remote_copy(
-            src_ref=q_send.at[chunk_of(j)], dst_ref=q_recv.at[chunk_of(j)],
+            src_ref=q_send.at[abl_of(j)], dst_ref=q_recv.at[abl_of(j)],
             send_sem=q_ssem.at[g], recv_sem=q_rsem.at[g],
             device_id=(ahead(me, j), mp), device_id_type=MESH,
         )
 
     def a_copy(g, j):
         return pltpu.make_async_remote_copy(
-            src_ref=a_send.at[chunk_of(j)], dst_ref=back.at[chunk_of(j)],
+            src_ref=a_send.at[abl_of(j)], dst_ref=back.at[abl_of(j)],
             send_sem=a_ssem.at[g], recv_sem=a_rsem.at[g],
             device_id=(behind(me, j), mp), device_id_type=MESH,
         )
@@ -310,13 +303,23 @@
         return carry
 
     lax.fori_loop(1, PEERS, send_meta, 0)
-    for c in loads[:3]:
-        c.wait()
+    loads[0].wait()
+
+    def regroup(b, carry):
+        src = pl.ds(pl.multiple_of(b * 64, 64), 64)
+        dst = pl.ds(pl.multiple_of((b * 64 + mp * W) % D, 64), 64)
+        w_v[:, dst, :] = jnp.swapaxes(w_raw[src], 0, 1)
+        return carry
 
     def head(i, carry):
         @pl.when(i < GROUPS)
         def _():
             gather(i)
+
+        @pl.when(i == 0)
+        def _():
+            loads[1].wait()
+            lax.fori_loop(0, D // 64, regroup, 0)
 
         @pl.when(i >= 1)
         def _():
@@ -332,7 +335,7 @@
 
     lax.fori_loop(0, GROUPS + 1, head, 0)
 
-    for c in loads[3:] + late:
+    for c in loads[2:]:
         c.wait()
     place = lax.broadcasted_iota(jnp.int32, (HLEN, W), 0).astype(F32)
     for user, length in ((0, len0), (1, len1)):
@@ -358,12 +361,13 @@
     def wait_group(buf, sem, g):
         @pl.when(g == 0)
         def _():
-            rows = pl.ds(CAP, GR - CAP)
+            rows = pl.ds(ABL, (GROUP-1)*ABL)
             pltpu.make_async_copy(buf.at[rows], buf.at[rows], sem.at[0]).wait()
 
         @pl.when(g > 0)
         def _():
-            pltpu.make_async_copy(buf.at[rows_of(g)], buf.at[rows_of(g)], sem.at[g]).wait()
+            rows = pl.ds(pl.multiple_of(g * GR, GR), GROUP * ABL)
+            pltpu.make_async_copy(buf.at[rows], buf.at[rows], sem.at[g]).wait()
 
     def body(i, carry):
         @pl.when(i < GROUPS)
@@ -423,6 +427,7 @@
         out_specs=vmem,
         scratch_shapes=[
             pltpu.VMEM((ROWS, W), BF16),
+            pltpu.VMEM((D, 4, W), BF16),
             pltpu.VMEM((4, D, W), BF16),
             pltpu.VMEM((D, W), BF16),
             pltpu.VMEM((2, HLEN, W), BF16),
@@ -449,7 +454,7 @@
             pltpu.VMEM((SLOTS, W), BF16),
             pltpu.VMEM((SLOTS, W), BF16),
             pltpu.VMEM((ROWS, W), F32),
-            dma((13,)),
+            dma((6,)),
             dma((GROUPS,)), dma((GROUPS,)),
             dma((GROUPS,)), dma((GROUPS,)),
             dma((GROUPS,)), dma((GROUPS,)),
@@ -458,7 +463,7 @@
             dma((GROUPS,)), dma((GROUPS,)),
         ],
         compiler_params=pltpu.CompilerParams(
-            collective_id=0, has_side_effects=True, vmem_limit_bytes=60 * 2**20
+            collective_id=0, has_side_effects=True, vmem_limit_bytes=VMEM_LIMIT
         ),
         cost_estimate=pl.CostEstimate(
             flops=20 * 10**9, bytes_accessed=10 * 10**6, transcendentals=9 * 10**6
@@ -471,8 +476,8 @@
         hist_len,
         k_cache,
         v_cache,
-        in_gain.reshape(2, W),
-        w_uvqk.transpose(1, 0, 2),
+        in_gain.reshape(1, D),
+        w_uvqk,
         attn_gain.reshape(1, W),
         w_out,
     )

time: 93.3 us -> 82.1 us (0.88); the launches traced: 93.1 us -> 80.5 us
  Pallas kernels: 84.6 us -> 78.2 us
  local copies, waits for them, and re-layouts: 8.5 us -> 2.26 us
    pallas_call x1, Pallas kernels: 84.6 us -> 78.2 us  [body(): pl.pallas_call(kernel, out_shape=jax.ShapeDtypeStruct((ROWS, W), BF16), i...]
    unnamed x2 -> x1, local copies, waits for them, and re-layouts: 7.21 us -> 2.26 us
    reshape x1 -> x0, local copies, waits for them, and re-layouts: 1.29 us -> none  [body(): in_gain.reshape(2, W)]
where the time goes in v2:
time: 82.1 us; the launch traced here: 80.5 us
  Pallas kernels  78.2 us (95%)
  local copies, waits for them, and re-layouts  2.26 us (3%)
    pallas_call x1, Pallas kernels, body(): pl.pallas_call(kernel, out_shape=jax.ShapeDtypeStruct((ROWS, W), BF16), i...  78.2 us
    unnamed x1, local copies, waits for them, and re-layouts  2.26 us

profile of v2, /device:TPU:1, one launch (start us, length us, event | category | flops | bytes accessed | tf_op | source)
XLA Modules:
  0.0 80.5 jit_solution(7658377786152641990)
XLA Ops:
  0.0 78.2 %routed_ranking.1 = bf16[1024,512]{1,0:T(8,128)(2,1)} custom-call(bf16[1024,512]{1,0:T(8,128)(2,1)} %x_hbm.1, s32[1,1024]{1,0:T(1,128)} %bitcast.4, s32[1,1024]{1,0:T(1,128)} %bitcast.5, s32[1,2]{1,0:T(1,128)} %hist_ref.1, bf16[2,512,512]{2,1,0:T(8,128)(2,1)} %k_hbm.1, bf16[2,512,512]{2,1,0:T(8,128)(2,1)} %v_hbm.1, f32[1,1024]{1,0:T(1,128)} %bitcast.6, ...), custom_call_target="tpu_custom_call" | custom-call | flops 20000000000 | bytes 10000000 | tf_op jit(solution)/shard_map/routed_ranking/pallas_call | solution.py:423
  78.2 2.3 %copy.12 = bf16[1024,512]{1,0:T(8,128)(2,1)} copy(bf16[1024,512]{1,0:T(8,128)(2,1)} %routed_ranking.1) | data formatting | bytes 2097152

commit v3 on v2

--- a/solution.py
+++ b/solution.py
@@ -22,9 +22,11 @@
 GROUP = 8
 GROUPS = PEERS // GROUP
 GR = GROUP * CAP
-STEP = 59
-STEP_INV = 51
-LAG = 4
+STEP = 37
+STEP_INV = 45
+LAG = 5
+HOLD = 2
+ORDER = 'EFG'
 EPS = 1e-05
 VMEM_LIMIT = 54 * 2**20
 ABL = CAP
@@ -67,7 +69,7 @@
 def kernel(
     x_hbm, dest_ref, slot_ref, hist_ref, k_hbm, v_hbm, in_gain_ref, w_hbm, attn_gain_ref, wout_hbm,
     out_ref,
-    x_v, w_raw, w_v, wout_v, k_v, v_v, v01, fs_row, fs_col, meta, metar, mask_in, inv_len, gain_v,
+    x_v, w_raw, w_v, wout_v, k_v, v_v, v01, fs_row, fs_col, meta, metar, theirs, mask_in, inv_len, gain_v,
     xs_own, xs_peer, h_v, q_send, q_recv, a_send, back, u_v, self_v, st_send, st_recv,
     y_own, y_peer, acc,
     load_sem, x_ssem, x_rsem, q_ssem, q_rsem, a_ssem, a_rsem, m_ssem, m_rsem, s_ssem, s_rsem,
@@ -125,19 +127,6 @@
     pos = jnp.concatenate(pos_parts, axis=1)
     fs = (number * CAP).astype(F32) + jnp.where(slot == 0, pos, (CAP - 1) - pos)
     fs_row[...] = jnp.broadcast_to(fs, (8, ROWS))
-    fs_col[...] = jnp.broadcast_to(fs, (HD, ROWS)).T
-    same = lax.broadcasted_iota(jnp.int32, (PEERS, ROWS), 0) == number
-    first = jnp.sum(jnp.where(same & (slot == 0), 1.0, 0.0), axis=1, keepdims=True)
-    hist = hist_ref[...].astype(F32)
-    len0, len1 = hist[:, 0:1], hist[:, 1:2]
-    lane = lax.broadcasted_iota(jnp.int32, (PEERS, HD), 1)
-    meta_rows = jnp.where(lane < 64, first, jnp.where(lane < 96, len0, len1))
-    meta[...] = meta_rows.reshape(PEERS, 1, HD)
-    metar[0] = meta[0]
-    gain_v[...] = jnp.concatenate(
-        [in_gain_ref[:, pl.ds(own_at, W)], in_gain_ref[:, pl.ds(peer_at, W)]], axis=1
-    )
-    acc[...] = jnp.zeros_like(acc)
 
     def rows_of(g):
         return pl.ds(pl.multiple_of(g * GR, GR), GR)
@@ -194,7 +183,6 @@
         slots = lax.broadcasted_iota(jnp.int32, (GR, ROWS), 0).astype(F32) + (g * GR).astype(F32)
         pick = jnp.where(slots == fs_row[0:1, :], 1.0, 0.0).astype(BF16)
         xs_own[rows_of(g), :] = jnp.dot(pick, x_v[...], preferred_element_type=F32).astype(BF16)
-        x_copy(g).start()
 
     def norm_and_query(g):
         x_copy(g).wait_recv()
@@ -296,14 +284,30 @@
         )
         acc[...] += jnp.dot(pick, fin, preferred_element_type=F32)
 
+    loads[0].wait()
+    gather(jnp.int32(0))
     pl.semaphore_wait(barrier, PEERS)
+    x_copy(0).start()
+
+    fs_col[...] = jnp.broadcast_to(fs, (HD, ROWS)).T
+    same = lax.broadcasted_iota(jnp.int32, (PEERS, ROWS), 0) == number
+    first = jnp.sum(jnp.where(same & (slot == 0), 1.0, 0.0), axis=1, keepdims=True)
+    hist = hist_ref[...].astype(F32)
+    len0, len1 = hist[:, 0:1], hist[:, 1:2]
+    lane = lax.broadcasted_iota(jnp.int32, (PEERS, HD), 1)
+    meta_rows = jnp.where(lane < 64, first, jnp.where(lane < 96, len0, len1))
+    meta[...] = meta_rows.reshape(PEERS, 1, HD)
+    metar[0] = meta[0]
+    gain_v[...] = jnp.concatenate(
+        [in_gain_ref[:, pl.ds(own_at, W)], in_gain_ref[:, pl.ds(peer_at, W)]], axis=1
+    )
+    acc[...] = jnp.zeros_like(acc)
 
     def send_meta(j, carry):
         m_copy(j).start()
         return carry
 
     lax.fori_loop(1, PEERS, send_meta, 0)
-    loads[0].wait()
 
     def regroup(b, carry):
         src = pl.ds(pl.multiple_of(b * 64, 64), 64)
@@ -311,29 +315,25 @@
         w_v[:, dst, :] = jnp.swapaxes(w_raw[src], 0, 1)
         return carry
 
+    loads[1].wait()
+    lax.fori_loop(0, D // 64, regroup, 0)
+
     def head(i, carry):
         @pl.when(i < GROUPS)
         def _():
             gather(i)
-
-        @pl.when(i == 0)
+            x_copy(i).start()
+
+        norm_and_query(i - 1)
+
+        @pl.when(i == 1)
         def _():
-            loads[1].wait()
-            lax.fori_loop(0, D // 64, regroup, 0)
-
-        @pl.when(i >= 1)
-        def _():
-            norm_and_query(i - 1)
-
-            @pl.when(i == 1)
-            def _():
-                q_recv[pl.ds(0, CAP), :] = q_send[pl.ds(0, CAP), :]
-
-            send_queries(i - 1)
-
+            q_recv[pl.ds(0, CAP), :] = q_send[pl.ds(0, CAP), :]
+
+        send_queries(i - 1)
         return carry
 
-    lax.fori_loop(0, GROUPS + 1, head, 0)
+    lax.fori_loop(1, GROUPS + 1, head, 0)
 
     for c in loads[2:]:
         c.wait()
@@ -346,17 +346,14 @@
     pltpu.make_async_copy(
         metar.at[pl.ds(1, PEERS - 1)], metar.at[pl.ds(1, PEERS - 1)], m_rsem.at[0]
     ).wait()
-    in_chunk = lax.broadcasted_iota(jnp.int32, (CAP, HD), 0).astype(F32)
-
-    def masks(j, carry):
-        mask_in[chunk_of(j), :] = jnp.where(in_chunk >= metar[j][:, 0:1], 1.0, 0.0)
-        theirs = metar[mirrored(j)]
-        l0, l1 = theirs[:, 64:65], theirs[:, 96:97]
-        length = jnp.where(in_chunk >= meta[j][:, 0:1], l1, l0)
-        inv_len[chunk_of(j), :] = 1.0 / (length + 1.0)
-        return carry
-
-    lax.fori_loop(0, PEERS, masks, 0)
+    for j in range(PEERS):
+        theirs[j] = metar[mirrored(j)]
+    in_chunk = lax.broadcasted_iota(jnp.int32, (PEERS, CAP, HD), 1).astype(F32)
+    mask_in[...] = jnp.where(in_chunk >= metar[...][:, :, 0:1], 1.0, 0.0).reshape(SLOTS, HD)
+    inv = 1.0 / (theirs[...] + 1.0)
+    inv_len[...] = jnp.where(
+        in_chunk >= meta[...][:, :, 0:1], inv[:, :, 96:97], inv[:, :, 64:65]
+    ).reshape(SLOTS, HD)
 
     def wait_group(buf, sem, g):
         @pl.when(g == 0)
@@ -380,20 +377,29 @@
             def _():
                 back[pl.ds(0, CAP), :] = a_send[pl.ds(0, CAP), :]
 
-            send_back(i)
-
-        @pl.when(jnp.logical_and(i >= LAG, i < GROUPS + LAG))
+        @pl.when(jnp.logical_and(i >= HOLD, i < GROUPS + HOLD))
         def _():
-            wait_group(back, a_rsem, i - LAG)
-            finish_sums(i - LAG)
-
-        @pl.when(jnp.logical_and(i >= LAG + 1, i < GROUPS + LAG + 1))
-        def _():
-            normalize(i - LAG - 1)
-
-        @pl.when(i >= LAG + 2)
-        def _():
-            output(i - LAG - 2)
+            send_back(i - HOLD)
+
+        def out_step():
+            @pl.when(jnp.logical_and(i >= LAG + 2, i < GROUPS + LAG + 2))
+            def _():
+                output(i - LAG - 2)
+
+        def norm_step():
+            @pl.when(jnp.logical_and(i >= LAG + 1, i < GROUPS + LAG + 1))
+            def _():
+                normalize(i - LAG - 1)
+
+        def sum_step():
+            @pl.when(jnp.logical_and(i >= LAG, i < GROUPS + LAG))
+            def _():
+                wait_group(back, a_rsem, i - LAG)
+                finish_sums(i - LAG)
+
+        steps = dict(E=sum_step, F=norm_step, G=out_step)
+        for name in ORDER:
+            steps[name]()
 
         return carry
 
@@ -435,6 +441,7 @@
             pltpu.VMEM((HEADS_HERE, HLEN, 2 * HD), BF16),
             pltpu.VMEM((8, ROWS), F32),
             pltpu.VMEM((ROWS, HD), F32),
+            pltpu.VMEM((PEERS, 1, HD), F32),
             pltpu.VMEM((PEERS, 1, HD), F32),
             pltpu.VMEM((PEERS, 1, HD), F32),
             pltpu.VMEM((SLOTS, HD), F32),

time: 82.1 us -> 76.1 us (0.927); the launches traced: 80.5 us -> 75.9 us
  Pallas kernels: 78.2 us -> 73.7 us
    pallas_call x1, Pallas kernels: 78.2 us -> 73.7 us  [body(): pl.pallas_call(kernel, out_shape=jax.ShapeDtypeStruct((ROWS, W), BF16), i...]
where the time goes in v3:
time: 76.1 us; the launch traced here: 75.9 us
  Pallas kernels  73.7 us (97%)
  local copies, waits for them, and re-layouts  2.26 us (3%)
    pallas_call x1, Pallas kernels, body(): pl.pallas_call(kernel, out_shape=jax.ShapeDtypeStruct((ROWS, W), BF16), i...  73.7 us
    unnamed x1, local copies, waits for them, and re-layouts  2.26 us

profile of v3, /device:TPU:1, one launch (start us, length us, event | category | flops | bytes accessed | tf_op | source)
XLA Modules:
  0.0 75.9 jit_solution(142189976066232752)
XLA Ops:
  0.0 73.7 %routed_ranking.1 = bf16[1024,512]{1,0:T(8,128)(2,1)} custom-call(bf16[1024,512]{1,0:T(8,128)(2,1)} %x_hbm.1, s32[1,1024]{1,0:T(1,128)} %bitcast.4, s32[1,1024]{1,0:T(1,128)} %bitcast.5, s32[1,2]{1,0:T(1,128)} %hist_ref.1, bf16[2,512,512]{2,1,0:T(8,128)(2,1)} %k_hbm.1, bf16[2,512,512]{2,1,0:T(8,128)(2,1)} %v_hbm.1, f32[1,1024]{1,0:T(1,128)} %bitcast.6, ...), custom_call_target="tpu_custom_call" | custom-call | flops 20000000000 | bytes 10000000 | tf_op jit(solution)/shard_map/routed_ranking/pallas_call | solution.py:429
  73.7 2.3 %copy.12 = bf16[1024,512]{1,0:T(8,128)(2,1)} copy(bf16[1024,512]{1,0:T(8,128)(2,1)} %routed_ranking.1) | data formatting | bytes 2097152

commit v4 on v3

--- a/solution.py
+++ b/solution.py
@@ -377,9 +377,14 @@
             def _():
                 back[pl.ds(0, CAP), :] = a_send[pl.ds(0, CAP), :]
 
-        @pl.when(jnp.logical_and(i >= HOLD, i < GROUPS + HOLD))
+        @pl.when(jnp.logical_and(i >= HOLD, i < GROUPS))
         def _():
             send_back(i - HOLD)
+
+        @pl.when(i == GROUPS - 1)
+        def _():
+            for g in range(GROUPS - HOLD, GROUPS):
+                send_back(jnp.int32(g))
 
         def out_step():
             @pl.when(jnp.logical_and(i >= LAG + 2, i < GROUPS + LAG + 2))

time: 76.1 us -> 75.2 us (0.988)
  Pallas kernels: 73.7 us -> 72.7 us
    pallas_call x1, Pallas kernels: 73.7 us -> 72.7 us  [body(): pl.pallas_call(kernel, out_shape=jax.ShapeDtypeStruct((ROWS, W), BF16), i...]
where the time goes in v4:
time: 75.2 us; the launch traced here: 75 us
  Pallas kernels  72.7 us (97%)
  local copies, waits for them, and re-layouts  2.26 us (3%)
    pallas_call x1, Pallas kernels, body(): pl.pallas_call(kernel, out_shape=jax.ShapeDtypeStruct((ROWS, W), BF16), i...  72.7 us
    unnamed x1, local copies, waits for them, and re-layouts  2.26 us

profile of v4, /device:TPU:1, one launch (start us, length us, event | category | flops | bytes accessed | tf_op | source)
XLA Modules:
  0.0 75.0 jit_solution(14963966069653555913)
XLA Ops:
  0.0 72.7 %routed_ranking.1 = bf16[1024,512]{1,0:T(8,128)(2,1)} custom-call(bf16[1024,512]{1,0:T(8,128)(2,1)} %x_hbm.1, s32[1,1024]{1,0:T(1,128)} %bitcast.4, s32[1,1024]{1,0:T(1,128)} %bitcast.5, s32[1,2]{1,0:T(1,128)} %hist_ref.1, bf16[2,512,512]{2,1,0:T(8,128)(2,1)} %k_hbm.1, bf16[2,512,512]{2,1,0:T(8,128)(2,1)} %v_hbm.1, f32[1,1024]{1,0:T(1,128)} %bitcast.6, ...), custom_call_target="tpu_custom_call" | custom-call | flops 20000000000 | bytes 10000000 | tf_op jit(solution)/shard_map/routed_ranking/pallas_call | solution.py:434
  72.7 2.3 %copy.12 = bf16[1024,512]{1,0:T(8,128)(2,1)} copy(bf16[1024,512]{1,0:T(8,128)(2,1)} %routed_ranking.1) | data formatting | bytes 2097152

commit v5 on v4

--- a/solution.py
+++ b/solution.py
@@ -25,7 +25,7 @@
 STEP = 37
 STEP_INV = 45
 LAG = 5
-HOLD = 2
+HOLD = 3
 ORDER = 'EFG'
 EPS = 1e-05
 VMEM_LIMIT = 54 * 2**20

time: 75.2 us -> 77.1 us (1.025)
  Pallas kernels: 72.7 us -> 74.5 us
    pallas_call x1, Pallas kernels: 72.7 us -> 74.5 us  [body(): pl.pallas_call(kernel, out_shape=jax.ShapeDtypeStruct((ROWS, W), BF16), i...]
where the time goes in v5:
time: 77.1 us; the launch traced here: 76.8 us
  Pallas kernels  74.5 us (97%)
  local copies, waits for them, and re-layouts  2.26 us (3%)
    pallas_call x1, Pallas kernels, body(): pl.pallas_call(kernel, out_shape=jax.ShapeDtypeStruct((ROWS, W), BF16), i...  74.5 us
    unnamed x1, local copies, waits for them, and re-layouts  2.26 us

profile of v5, /device:TPU:1, one launch (start us, length us, event | category | flops | bytes accessed | tf_op | source)
XLA Modules:
  0.0 76.8 jit_solution(2399569329970285404)
XLA Ops:
  0.0 74.5 %routed_ranking.1 = bf16[1024,512]{1,0:T(8,128)(2,1)} custom-call(bf16[1024,512]{1,0:T(8,128)(2,1)} %x_hbm.1, s32[1,1024]{1,0:T(1,128)} %bitcast.4, s32[1,1024]{1,0:T(1,128)} %bitcast.5, s32[1,2]{1,0:T(1,128)} %hist_ref.1, bf16[2,512,512]{2,1,0:T(8,128)(2,1)} %k_hbm.1, bf16[2,512,512]{2,1,0:T(8,128)(2,1)} %v_hbm.1, f32[1,1024]{1,0:T(1,128)} %bitcast.6, ...), custom_call_target="tpu_custom_call" | custom-call | flops 20000000000 | bytes 10000000 | tf_op jit(solution)/shard_map/routed_ranking/pallas_call | solution.py:434
  74.5 2.3 %copy.12 = bf16[1024,512]{1,0:T(8,128)(2,1)} copy(bf16[1024,512]{1,0:T(8,128)(2,1)} %routed_ranking.1) | data formatting | bytes 2097152
